TPU v7x, 32 devices: a whole 2x2x4 slice. The times are simulated.
32 devices in a mesh: segment: 2 (over core), dp: 8 (over z, x), mp: 2 (over y).
Axes of the slice: x: 2, y: 2, z: 4, core: 2. Of those that a mesh axis runs over, the one named last changes fastest.
Arguments:
- grad_top: bfloat16 [4096, 2048], P('dp'), may hold values from -6 to 6
- saved_query: bfloat16 [2, 4096, 2048], P('segment', 'dp', 'mp'), may hold values from -12 to 12
- saved_key: bfloat16 [2, 6144, 2048], P('segment', 'dp', 'mp'), may hold values from -4 to 4
- saved_value: bfloat16 [2, 6144, 2048], P('segment', 'dp', 'mp'), may hold values from -6 to 6
- w_query: bfloat16 [2, 2048, 2048], P('segment', 'mp', 'dp'), may hold values from -0.125 to 0.125
- w_key: bfloat16 [2, 2048, 2048], P('segment', 'mp', 'dp'), may hold values from -0.125 to 0.125
- w_value: bfloat16 [2, 2048, 2048], P('segment', 'mp', 'dp'), may hold values from -0.125 to 0.125
- w_out: bfloat16 [2, 2048, 2048], P('segment', 'mp', 'dp'), may hold values from -0.125 to 0.125
- query_length: int32 [16, 2], P('dp'), may hold values from 64 to 128
- key_offset: int32 [16, 2], P('dp'), may hold values from 0 to 2, as said below
- key_length: int32 [16, 2], P('dp'), may hold values from 64 to 256
- tile_owner: int32 [16, 3], replicated, may hold values from 0 to 47, as said below
Outputs:
- section_grads: bfloat16 [2, 4096, 2048], P('segment', 'dp', 'mp')
- encoder_grads: bfloat16 [6144, 2048], P('dp', ('segment', 'mp'))
Inputs may be any that keep to these rules, and one draw needn't show every extreme that they name: Example 0 takes tiles 0 to key_offset[s, 1] - 1 and example 1 the rest of the sequence's encoder tiles; each example holds at least one tile and its rows fit in its tiles. `tile_owner`: every global tile appears once. Tile t is owned by dp index t // 6; the owner of a tile of dp index i (sequences i * 2 to i * 2 + 1) is i - 1, i or i + 1, wrapping around. Each dp index hands 1 to 2 tiles to each neighbour, and 2 is reached in every draw.
All inputs are finite; a program needn't handle non-finite values.
Results may differ from a plain program's by a relative error of at most 0.019.
Values may be sent and summed in bfloat16 or wider, within the bound.
A program may use at most 128 MiB of HBM per device.

v0:
```python
import functools

import jax
import jax.numpy as jnp
from jax import lax
from jax.experimental import pallas as pl
from jax.experimental.pallas import tpu as pltpu
from jax.sharding import PartitionSpec as P

DH = 256
TILE = 128
CAP = 2
BLOCK = 256
masked_floor = -1e30
BF16, F32 = jnp.bfloat16, jnp.float32


def dot(a, b, ca, cb):
    return lax.dot_general(a, b, (((ca,), (cb,)), ((), ())), preferred_element_type=F32)


def tick_kernel(count, half, sc, g_ref, q_ref, k_ref, v_ref, *rest):
    wo, wq = rest[:count], rest[count : 2 * count]
    mixed_ref, kg_ref, vg_ref, acc = rest[2 * count :]
    head = pl.program_id(0)
    per = half // BLOCK
    scale = DH ** (-0.5)

    def place(b):
        src = sc[b]
        return src // per, pl.ds(pl.multiple_of((src % per) * BLOCK, BLOCK), BLOCK)

    og = None
    for b in range(count):
        at, cols = place(b)
        term = dot(g_ref[at, :, cols], wo[b][...], 1, 1)
        og = term if og is None else og + term
    og = og.astype(BF16)
    q, k, v = q_ref[0], k_ref[0], v_ref[0]
    scores = dot(q, k, 1, 1) * scale
    rows = lax.broadcasted_iota(jnp.int32, scores.shape, 0)
    cols_id = lax.broadcasted_iota(jnp.int32, scores.shape, 1)
    allowed = None
    for e in range(2):
        q_len, k_off, k_len = sc[count + e], sc[count + 2 + e] * TILE, sc[count + 4 + e]
        hit = (rows >= e * TILE) & (rows < e * TILE + q_len)
        hit = hit & (cols_id >= k_off) & (cols_id < k_off + k_len)
        allowed = hit if allowed is None else allowed | hit
    masked = jnp.where(allowed, scores, masked_floor)
    top = jnp.max(masked, axis=-1, keepdims=True)
    terms = jnp.where(allowed, jnp.exp(masked - top), 0.0)
    prob = terms / jnp.maximum(jnp.sum(terms, axis=-1, keepdims=True), 1.0)
    prob_bf = prob.astype(BF16)
    attended = dot(prob_bf, v, 1, 0)
    out_dot = jnp.sum(og.astype(F32) * attended, axis=-1, keepdims=True)
    sg = (prob * (dot(og, v, 1, 1) - out_dot)).astype(BF16)
    qg = (dot(sg, k, 1, 0) * scale).astype(BF16)
    kg_ref[...] = (dot(sg, q, 0, 0) * scale).astype(BF16)
    vg_ref[...] = dot(prob_bf, og, 0, 0).astype(BF16)

    @pl.when(head == 0)
    def _():
        acc[...] = jnp.zeros_like(acc)

    for b in range(count):
        at, cols = place(b)
        acc[at, :, cols] += dot(qg, wq[b][...], 1, 0)

    @pl.when(head == pl.num_programs(0) - 1)
    def _():
        mixed_ref[...] = acc[...].astype(BF16)


def run_tick(scalars, grad, at, seq, saved_q, saved_k, saved_v, wo, wq, q_rows, k_rows):
    half = grad.shape[2]
    heads = saved_q.shape[2] // DH
    count = len(wo)
    weight = pl.BlockSpec((DH, BLOCK), lambda h, sc: (h, 0))
    macs = heads * q_rows * DH * (4 * half + 6 * k_rows)
    return pl.pallas_call(
        functools.partial(tick_kernel, count, half),
        grid_spec=pltpu.PrefetchScalarGridSpec(
            num_scalar_prefetch=1,
            grid=(heads,),
            in_specs=[
                pl.BlockSpec((2, q_rows, half), lambda h, sc: (0, at, 0)),
                pl.BlockSpec((1, q_rows, DH), lambda h, sc: (0, seq, h)),
                pl.BlockSpec((1, k_rows, DH), lambda h, sc: (0, seq, h)),
                pl.BlockSpec((1, k_rows, DH), lambda h, sc: (0, seq, h)),
            ]
            + [weight] * (2 * count),
            out_specs=[
                pl.BlockSpec((2, q_rows, half), lambda h, sc: (0, 0, 0)),
                pl.BlockSpec((k_rows, DH), lambda h, sc: (0, h)),
                pl.BlockSpec((k_rows, DH), lambda h, sc: (0, h)),
            ],
            scratch_shapes=[pltpu.VMEM((2, q_rows, half), F32)],
        ),
        out_shape=[
            jax.ShapeDtypeStruct((2, q_rows, half), BF16),
            jax.ShapeDtypeStruct((k_rows, heads * DH), BF16),
            jax.ShapeDtypeStruct((k_rows, heads * DH), BF16),
        ],
        compiler_params=pltpu.CompilerParams(vmem_limit_bytes=40 << 20),
        cost_estimate=pl.CostEstimate(
            flops=2 * macs, bytes_accessed=16 << 20, transcendentals=heads * q_rows * k_rows
        ),
    )(scalars, grad, saved_q, saved_k, saved_v, *wo, *wq)


def encoder_kernel(count, quarter, sc, kg_ref, vg_ref, *rest):
    wk, wv, out_ref = rest[:count], rest[count : 2 * count], rest[2 * count]
    per = quarter // BLOCK
    kg, vg = kg_ref[...], vg_ref[...]
    for b in range(count):
        src = sc[b]
        cols = pl.ds(pl.multiple_of((src % per) * BLOCK, BLOCK), BLOCK)
        part = dot(kg, wk[b][...], 1, 0) + dot(vg, wv[b][...], 1, 0)
        out_ref[src // per, :, cols] = part.astype(BF16)


def run_encoder(scalars, kg, vg, wk, wv):
    count = len(wk)
    rows, depth = kg.shape
    quarter = count * BLOCK // 4
    step = 256
    whole = pl.BlockSpec((depth, BLOCK), lambda i, sc: (0, 0))
    return pl.pallas_call(
        functools.partial(encoder_kernel, count, quarter),
        grid_spec=pltpu.PrefetchScalarGridSpec(
            num_scalar_prefetch=1,
            grid=(rows // step,),
            in_specs=[pl.BlockSpec((step, depth), lambda i, sc: (i, 0))] * 2
            + [whole] * (2 * count),
            out_specs=pl.BlockSpec((4, step, quarter), lambda i, sc: (0, i, 0)),
        ),
        out_shape=jax.ShapeDtypeStruct((4, rows, quarter), BF16),
        compiler_params=pltpu.CompilerParams(vmem_limit_bytes=48 << 20),
        cost_estimate=pl.CostEstimate(
            flops=16 * rows * depth * quarter, bytes_accessed=14 << 20, transcendentals=0
        ),
    )(scalars, kg, vg, *wk, *wv)


def pick_kernel(sc, local_ref, left_ref, right_ref):
    for c in range(CAP):
        left_ref[c] = local_ref[sc[c]]
        right_ref[c] = local_ref[sc[CAP + c]]


def place_kernel(sc, left_ref, local_ref, right_ref, out_ref):
    tiles = local_ref.shape[0]
    for s in range(tiles):
        i = sc[s]

        @pl.when(i < CAP)
        def _():
            out_ref[s] = left_ref[jnp.minimum(i, CAP - 1)]

        @pl.when((i >= CAP) & (i < CAP + tiles))
        def _():
            out_ref[s] = local_ref[jnp.clip(i - CAP, 0, tiles - 1)]

        @pl.when(i >= CAP + tiles)
        def _():
            out_ref[s] = right_ref[jnp.clip(i - CAP - tiles, 0, CAP - 1)]


def small_call(body, scalars, arrays, outs):
    vmem = pl.BlockSpec(memory_space=pltpu.VMEM)
    single = not isinstance(outs, list)
    return pl.pallas_call(
        body,
        in_specs=[pl.BlockSpec(memory_space=pltpu.SMEM)] + [vmem] * len(arrays),
        out_specs=vmem if single else [vmem] * len(outs),
        out_shape=outs,
        compiler_params=pltpu.CompilerParams(vmem_limit_bytes=24 << 20),
    )(scalars, *arrays)


def gathered(shard):
    full = lax.all_gather(shard, "dp", axis=1, tiled=True)
    blocks = [full[:, i : i + BLOCK] for i in range(0, full.shape[1], BLOCK)]
    return blocks, list(jnp.arange(len(blocks), dtype=jnp.int32))


def chain_kernel(dims, sc, own, top_hbm, q_hbm, k_hbm, v_hbm, wo_hbm, wq_hbm, wk_hbm, wv_hbm,
                 sections_ref, out_ref,
                 wbuf, g, q_ref, k_ref, v_ref, acc, qg, kg, vg, mixed, other, parts, near, fwd, far,
                 kg_in, vg_in, lent, lent_in, back, loc, inc, snd,
                 ldw, ldg, ldq, zs, zr, xs, xr, ms, mr, gs, gr, ks, kr, ps, pr, ys, yr,
                 us, ur, rs, rr, hs, hr, gate):
    q_rows, k_rows, heads, devices = dims
    depth = heads * DH
    scale = DH ** (-0.5)
    seg, me, mp = lax.axis_index("segment"), lax.axis_index("dp"), lax.axis_index("mp")
    z, x = me // 2, me % 2
    side = z // 2
    mesh_id = pl.DeviceIdType.MESH
    plane = {"e": 3 * side, "m": 1 + side, "n": 2 - side, "f": 3 - 3 * side}
    blk = {c: plane[c] * 2 + x for c in plane}
    blk.update({"p" + c: plane[c] * 2 + 1 - x for c in plane})
    at_end = (z == 0) | (z == 3)
    side_peer, cross, core = (seg, z * 2 + 1 - x, mp), (seg, me, 1 - mp), (1 - seg, me, mp)
    diag = jnp.where(x == 0, (me + devices - 1) % devices, (me + 1) % devices)
    end_peer, mid_peer = (seg, plane["e"] * 2 + x, mp), (seg, plane["m"] * 2 + x, mp)
    far_mid = (seg, plane["n"] * 2 + x, mp)
    upper, lower = pl.ds(0, depth // 2), pl.ds(depth // 2, depth // 2)
    whole = pl.ds(0, depth)
    step = 256

    def load(src, dst, sem):
        return pltpu.make_async_copy(src, dst, sem)

    weights = (wo_hbm, wq_hbm, wk_hbm, wv_hbm)
    w_loads = [load(weights[u].at[0], wbuf.at[u, me], ldw.at[u]) for u in range(4)]
    in_loads = [load(a.at[0], b, ldq.at[i])
                for i, (a, b) in enumerate(((q_hbm, q_ref), (k_hbm, k_ref), (v_hbm, v_ref)))]

    def g_load(b):
        cols = pl.ds(pl.multiple_of(b * BLOCK, BLOCK), BLOCK)
        return load(top_hbm.at[:, cols], g.at[b], ldg.at[b])

    w_loads[0].start()

    barrier = pltpu.get_barrier_semaphore()

    def greet(peers):
        for peer in peers:
            pl.semaphore_signal(barrier, inc=1, device_id=peer, device_id_type=mesh_id)

    all_peers = [side_peer, cross, core, (seg, diag, mp)]
    greet(all_peers)

    @pl.when(at_end)
    def _():
        greet([mid_peer])

        @pl.when(seg == 0)
        def _():
            greet([(1, plane["m"] * 2 + x, mp)])

    @pl.when(jnp.logical_not(at_end))
    def _():
        greet([end_peer, far_mid])

        @pl.when(seg == 1)
        def _():
            greet([(0, plane["e"] * 2 + x, mp)])

    @pl.when(seg == 1)
    def _():
        for b in range(8):
            g_load(b).start()

    for c in w_loads[1:] + in_loads:
        c.start()
    for c in w_loads:
        c.wait()

    pl.semaphore_wait(barrier, jnp.where(at_end, 6 - seg, 6 + seg))

    def loop(rows, body):
        def one(i, carry):
            body(pl.ds(pl.multiple_of(i * step, step), step))
            return carry

        lax.fori_loop(0, rows // step, one, 0)

    def each(names, body):
        ids = [blk[n] for n in names]

        def one(i, carry):
            b = ids[0]
            for j in range(1, len(ids)):
                b = jnp.where(i == j, ids[j], b)
            body(b)
            return carry

        if len(ids) == 1:
            body(ids[0])
        else:
            lax.fori_loop(0, len(ids), one, 0)

    class Role:
        def __init__(self, end, layer):
            self.end, self.layer = end, layer
            self.pending = []
            self.started = False
            upper_end = end and layer == 1
            self.makers = [self.mixed_copy, self.far_copy, self.left_copy, self.right_copy]
            if layer == 1:
                self.makers.append(self.section_copy)
            if not upper_end:
                self.makers.append(self.part_copy)
            if layer == 1 and not end:
                self.makers += [self.lent_copy, self.back_copy]


        def send(self, src, dst, a, b, peer, cond=None):
            copy = pltpu.make_async_remote_copy(
                src_ref=src, dst_ref=dst, send_sem=a, recv_sem=b, device_id=peer, device_id_type=mesh_id
            )
            self.pending.append((cond, copy))
            if cond is None:
                copy.start()
            else:
                pl.when(cond)(copy.start)

        def recv(self, dst, a, b):
            pltpu.make_async_remote_copy(
                src_ref=dst, dst_ref=dst, send_sem=a, recv_sem=b, device_id=side_peer,
                device_id_type=mesh_id,
            ).wait_recv()

        def remote(self, src, dst, a, b, peer):
            return pltpu.make_async_remote_copy(
                src_ref=src, dst_ref=dst, send_sem=a, recv_sem=b, device_id=peer, device_id_type=mesh_id
            )

        def finish(self):
            for _, copy in self.pending:
                copy.wait_send()

            def one(b, carry):
                for make in self.makers:
                    copy, cond = make(b)
                    if cond is None:
                        copy.wait_send()
                    else:
                        pl.when(cond)(copy.wait_send)
                return carry

            lax.fori_loop(0, 8, one, 0)

        def start(self, make, b):
            copy, cond = make(b)
            if cond is None:
                copy.start()
            else:
                pl.when(cond)(copy.start)

        def w(self, u, name, rows=whole):
            return wbuf.at[u, blk[name], rows]

        def zsend(self, kind, u, name, peer, rows=whole):
            ref = self.w(u, name, rows)
            self.send(ref, ref, zs.at[kind, u], zr.at[kind, u], peer)

        def zrecv(self, kind, u, name, rows=whole):
            self.recv(self.w(u, name, rows), zs.at[kind, u], zr.at[kind, u])

        def lent_unit(self, u):
            return self.layer == 1 and u >= 2

        def x_rows(self, u, name):
            if name != "f":
                return whole
            if self.end:
                return lower if u < 2 else whole
            return whole if self.lent_unit(u) else lower

        def xsend(self, u, name):
            ref = self.w(u, name, self.x_rows(u, name))
            i = "emnf".index(name)
            self.send(ref, ref, xs.at[i, u], xr.at[i, u], side_peer)

        def xrecv(self, u, name):
            i = "emnf".index(name)
            self.recv(self.w(u, "p" + name, self.x_rows(u, name)), xs.at[i, u], xr.at[i, u])

        def A(self, u):
            if self.end:
                self.zsend(0, u, "e", mid_peer)
                if not self.lent_unit(u):
                    self.xsend(u, "e")
            else:
                if not self.lent_unit(u):
                    self.zsend(2, u, "m", end_peer)
                self.zsend(6, u, "m", far_mid)
                self.xsend(u, "m")

        def Be(self, u):
            self.zrecv(0, u, "e")
            self.zsend(7, u, "e", far_mid)
            if self.lent_unit(u):
                self.xsend(u, "e")

        def Bp(self, u):
            if self.end:
                self.xrecv(u, "e")
                self.zsend(1, u, "pe", mid_peer)
            elif not self.lent_unit(u):
                self.zrecv(1, u, "pe")
                self.zsend(8, u, "pe", far_mid, upper)

        def Cm(self, u):
            self.zrecv(2, u, "m")
            self.xsend(u, "m")

        def C(self, u):
            if self.end:
                self.zrecv(3, u, "n")
                self.xsend(u, "n")
            else:
                self.zrecv(6, u, "n")
                if not self.lent_unit(u):
                    self.zsend(3, u, "n", end_peer)
                self.xsend(u, "n")

        def Df(self, u):
            if self.end:
                self.zrecv(4, u, "f")
            else:
                self.zrecv(7, u, "f")
                if not self.lent_unit(u):
                    self.zsend(4, u, "f", end_peer)
            self.xsend(u, "f")

        def Dp(self, u):
            if self.end:
                if u < 2:
                    self.zrecv(5, u, "pf", upper)
            elif not self.lent_unit(u):
                self.zrecv(8, u, "pf", upper)
                if u < 2:
                    self.zsend(5, u, "pf", end_peer, upper)


        def mixed_copy(self, b):
            return (self.remote(mixed.at[b], other.at[b], ms.at[b], mr.at[b], cross),
                    None if self.layer == 1 else b // 4 != mp)

        def section_copy(self, b):
            return self.remote(g.at[b], g.at[b], gs.at[b], gr.at[b], core), None

        def part_copy(self, b):
            return (self.remote(parts.at[b], near.at[b % 4], ps.at[b], pr.at[b], core),
                    b // 4 != self.layer)

        def lent_copy(self, b):
            i = (b // 4) * 2 + b % 2
            return (self.remote(lent.at[b], lent_in.at[i], us.at[i], ur.at[i], cross),
                    (b // 2) % 2 != mp)

        def back_copy(self, b):
            i, j = (b // 4) * 2 + b % 2, b % 2
            return (self.remote(lent.at[b], back.at[j], rs.at[i], rr.at[j],
                                (b // 4, plane["e"] * 2 + x, mp)), (b // 2) % 2 == mp)

        def onward(self, b):
            return (b // 4 == self.layer) & ((b // 2) % 2 != mp)

        def mine(self, b):
            return (b // 4 == self.layer) & ((b // 2) % 2 == mp)

        def far_copy(self, b):
            j = b % 2
            if self.end:
                src = parts.at[b] if self.layer == 0 else near.at[b % 4]
            else:
                src = fwd.at[j]
            return self.remote(src, far.at[j], ys.at[j], yr.at[j], cross), self.onward(b)

        def left_copy(self, b):
            j = b % 2
            return (self.remote(snd.at[j, pl.ds(0, CAP)], inc.at[j, pl.ds(CAP, CAP)], hs.at[j, 0],
                                hr.at[j, 0], (seg, (me + devices - 1) % devices, mp)), self.mine(b))

        def right_copy(self, b):
            j = b % 2
            return (self.remote(snd.at[j, pl.ds(CAP, CAP)], inc.at[j, pl.ds(0, CAP)], hs.at[j, 1],
                                hr.at[j, 1], (seg, (me + 1) % devices, mp)), self.mine(b))


        def out_blocks(self, names):
            if not self.started:
                acc[...] = jnp.zeros_like(acc)
            self.started = True

            def block(b):
                if self.layer == 1:
                    g_load(b).wait()
                else:
                    self.recv(g.at[b], gs.at[b], gr.at[b])

                def body(rows):
                    acc[rows, :] += dot(g[b, rows, :], wbuf[0, b], 1, 1)

                loop(2 * q_rows, body)

            each(names, block)

        def attend(self):
            rows = lax.broadcasted_iota(jnp.int32, (k_rows, q_rows), 1)
            cols = lax.broadcasted_iota(jnp.int32, (k_rows, q_rows), 0)

            def one_sequence(s, carry):
                qr = pl.ds(pl.multiple_of(s * q_rows, q_rows), q_rows)
                kr_ = pl.ds(pl.multiple_of(s * k_rows, k_rows), k_rows)
                allowed = None
                for e in range(2):
                    q_len, k_off, k_len = sc[s, e], sc[s, 2 + e] * TILE, sc[s, 4 + e]
                    hit = (rows >= e * TILE) & (rows < e * TILE + q_len)
                    hit = hit & (cols >= k_off) & (cols < k_off + k_len)
                    allowed = hit if allowed is None else allowed | hit

                def one_head(h, carry):
                    hd = pl.ds(pl.multiple_of(h * DH, DH), DH)
                    og = acc[qr, hd].astype(BF16)
                    q, k, v = q_ref[qr, hd], k_ref[kr_, hd], v_ref[kr_, hd]
                    masked = jnp.where(allowed, dot(k, q, 1, 1) * scale, masked_floor)
                    change = dot(v, og, 1, 1)
                    peak = jnp.maximum(jnp.max(masked, axis=0, keepdims=True), masked_floor / 2)
                    terms = jnp.exp(masked - peak)
                    prob = terms * (1.0 / jnp.maximum(jnp.sum(terms, axis=0, keepdims=True), 1.0))
                    prob_bf = prob.astype(BF16)
                    out_dot = jnp.sum(prob_bf.astype(F32) * change, axis=0, keepdims=True)
                    sg = (prob * (change - out_dot)).astype(BF16)
                    vg[kr_, hd] = dot(prob_bf, og, 1, 0).astype(BF16)
                    kg[kr_, hd] = (dot(sg, q, 1, 0) * scale).astype(BF16)
                    qg[qr, hd] = (dot(sg, k, 0, 0) * scale).astype(BF16)
                    return carry

                return lax.fori_loop(0, heads, one_head, carry)

            lax.fori_loop(0, 2, one_sequence, 0)

        def query_blocks(self, names):
            def block(b):
                def body(rows):
                    mixed[b, rows, :] = dot(qg[rows, :], wbuf[1, b], 1, 0).astype(BF16)

                loop(2 * q_rows, body)
                self.start(self.mixed_copy, b)

            each(names, block)

        def section_blocks(self, names):
            def total(b, rows):
                change = mixed[b, rows, :].astype(F32) + other[b, rows, :].astype(F32)
                return (g[b, rows, :].astype(F32) + change).astype(BF16)

            def block(b):
                cols = pl.ds(pl.multiple_of((b % 4) * BLOCK, BLOCK), BLOCK)
                if self.layer == 1:
                    self.recv(other.at[b], ms.at[b], mr.at[b])

                    def body(rows):
                        g[b, rows, :] = total(b, rows)

                    loop(2 * q_rows, body)
                    self.start(self.section_copy, b)

                @pl.when(b // 4 == mp)
                def _():
                    if self.layer == 0:
                        self.recv(other.at[b], ms.at[b], mr.at[b])

                    def body(rows):
                        sections_ref[0, rows, cols] = (
                            g[b, rows, :] if self.layer == 1 else total(b, rows)
                        )

                    loop(2 * q_rows, body)

            each(names, block)

        def project(self, kref, vref, dst, b):
            def body(rows):
                part = dot(kref[rows, :], wbuf[2, b], 1, 0) + dot(vref[rows, :], wbuf[3, b], 1, 0)
                dst[b, rows, :] = part.astype(BF16)

            loop(2 * k_rows, body)

        def encode(self, names):
            def block(b):
                self.project(kg, vg, parts, b)
                self.start(self.part_copy, b)

            each(names, block)

        def encode_lent(self, names):
            def block(b):
                self.project(kg_in, vg_in, lent, b)
                self.start(self.lent_copy, b)

            each(names, block)

        def give_back(self, names):
            def block(b):
                i = (b // 4) * 2 + b % 2

                @pl.when((b // 2) % 2 == mp)
                def _():
                    self.recv(lent_in.at[i], us.at[i], ur.at[i])

                    def body(rows):
                        both = lent[b, rows, :].astype(F32) + lent_in[i, rows, :].astype(F32)
                        lent[b, rows, :] = both.astype(BF16)

                    loop(2 * k_rows, body)

                self.start(self.back_copy, b)

            each(names, block)

        def reduce_cores(self, names):
            def block(b):
                if not (self.end and self.layer == 0):

                    @pl.when(b // 4 == self.layer)
                    def _():
                        self.recv(near.at[b % 4], ps.at[b], pr.at[b])

                if not self.end:

                    @pl.when(self.onward(b))
                    def _():
                        def body(rows):
                            both = parts[b, rows, :].astype(F32) + near[b % 4, rows, :].astype(F32)
                            fwd[b % 2, rows, :] = both.astype(BF16)

                        loop(2 * k_rows, body)

                self.start(self.far_copy, b)

            each(names, block)

        def reduce_heads(self, names):
            def block(b):
                j = b % 2

                @pl.when(self.mine(b))
                def _():
                    self.recv(far.at[j], ys.at[j], yr.at[j])
                    if self.end:
                        self.recv(back.at[j], rs.at[j], rr.at[j])

                    def body(t, carry):
                        rows = pl.ds(pl.multiple_of(t * TILE, TILE), TILE)
                        total = far[j, rows, :].astype(F32)
                        if self.end:
                            total += back[j, rows, :].astype(F32)
                        if not (self.end and self.layer == 1):
                            total += parts[b, rows, :].astype(F32)
                        if not (self.end and self.layer == 0):
                            total += near[b % 4, rows, :].astype(F32)
                        loc[j, t] = total.astype(BF16)
                        return carry

                    lax.fori_loop(0, 2 * k_rows // TILE, body, 0)
                    for c in range(CAP):
                        snd[j, c] = loc[j, pick_left[c]]
                        snd[j, CAP + c] = loc[j, pick_right[c]]

                self.start(self.left_copy, b)
                self.start(self.right_copy, b)

            each(names, block)

        def place(self):
            for j in range(2):
                self.recv(inc.at[j, pl.ds(CAP, CAP)], hs.at[j, 0], hr.at[j, 0])
                self.recv(inc.at[j, pl.ds(0, CAP)], hs.at[j, 1], hr.at[j, 1])
            for j in range(2):
                for t in range(tiles):
                    i = take[t]
                    kept = loc[j, jnp.minimum(i, tiles - 1)]
                    came = inc[j, jnp.clip(i - tiles, 0, 2 * CAP - 1)]
                    out_ref[t * TILE : (t + 1) * TILE, j * BLOCK : (j + 1) * BLOCK] = jnp.where(
                        i < tiles, kept, came
                    )

    tiles = 2 * k_rows // TILE
    per = tiles // 2

    def globals_of(source):
        return [own[source * 2 + t // per, t % per] for t in range(tiles)]

    def picks(goes, to):
        seen, chosen = jnp.int32(0), [jnp.int32(0)] * CAP
        for t in range(tiles):
            hit = (goes[t] >= to * tiles) & (goes[t] < (to + 1) * tiles)
            chosen = [jnp.where(hit & (seen == c), t, chosen[c]) for c in range(CAP)]
            seen = seen + hit.astype(jnp.int32)
        return chosen

    left_of, right_of = (me + devices - 1) % devices, (me + 1) % devices
    mine_goes = globals_of(me)
    pick_left, pick_right = picks(mine_goes, left_of), picks(mine_goes, right_of)
    take = [jnp.int32(0)] * tiles
    for source, base in ((me, 0), (left_of, tiles), (right_of, tiles + CAP)):
        goes = mine_goes if base == 0 else globals_of(source)
        seen = jnp.int32(0)
        for t in range(tiles):
            slot = goes[t] - me * tiles
            hit = (slot >= 0) & (slot < tiles)
            value = t if base == 0 else base + seen
            take = [jnp.where(slot == s, value, take[s]) for s in range(tiles)]
            seen = seen + hit.astype(jnp.int32)

    def mid_upper():
        r = Role(False, 1)
        r.A(0)
        r.Be(0)
        r.C(0)
        pl.semaphore_signal(gate, inc=1, device_id=core, device_id_type=mesh_id)
        r.xrecv(0,"m")
        r.out_blocks(["m", "e", "n", "pm"])
        r.Bp(0)
        r.A(1)
        r.Df(0)
        r.xrecv(0,"n")
        r.out_blocks(["pe", "pn", "f"])
        r.Be(1)
        r.Dp(0)
        r.C(1)
        r.Bp(1)
        r.xrecv(0,"f")
        r.out_blocks(["pf"])
        for c in in_loads:
            c.wait()
        r.attend()
        r.Df(1)
        r.Dp(1)
        r.A(2)
        r.A(3)
        r.Be(2)
        r.Be(3)
        r.xrecv(1,"m")
        r.query_blocks(["m", "e", "n", "pm"])
        r.xrecv(1,"n")
        r.query_blocks(["pe", "pn", "f"])
        r.xrecv(1,"f")
        r.query_blocks(["pf"])
        r.C(2)
        r.C(3)
        r.section_blocks(["m", "e", "n", "pm"])
        r.Df(2)
        r.section_blocks(["pe", "pn", "f"])
        r.section_blocks(["pf"])
        r.Df(3)
        r.xrecv(2,"m")
        r.xrecv(3,"m")
        r.xrecv(2,"e")
        r.xrecv(3,"e")
        r.xrecv(2,"n")
        r.xrecv(3,"n")
        r.encode(["m", "e", "n", "pm", "pe", "pn"])
        r.recv(kg_in, ks.at[0], kr.at[0])
        r.recv(vg_in, ks.at[1], kr.at[1])
        r.encode_lent(["m", "e", "n", "pm", "pe", "pn"])
        r.xrecv(2,"f")
        r.xrecv(3,"f")
        r.encode(["f", "pf"])
        r.encode_lent(["f", "pf"])
        r.give_back(["m", "e", "n", "pm", "pe", "pn"])
        r.reduce_cores(["m", "e", "n", "pm"])
        r.reduce_cores(["f"])
        r.give_back(["f", "pf"])
        r.reduce_cores(["pe", "pn"])
        r.reduce_cores(["pf"])
        r.reduce_heads(["m", "e", "n", "pm"])
        r.reduce_heads(["f"])
        r.reduce_heads(["pe", "pn"])
        r.reduce_heads(["pf"])
        r.place()
        r.finish()

    def mid_lower():
        r = Role(False, 0)
        pl.semaphore_wait(gate, 1)
        r.A(0)
        r.C(0)
        r.Be(0)
        r.Df(0)
        r.A(1)
        r.Be(1)
        r.Bp(0)
        r.xrecv(0,"m")
        r.xrecv(0,"n")
        r.out_blocks(["m", "e", "n", "pm", "pe", "pn"])
        r.Bp(1)
        r.C(1)
        r.Df(1)
        r.A(3)
        r.Dp(0)
        r.xrecv(0,"f")
        r.out_blocks(["f", "pf"])
        for c in in_loads:
            c.wait()
        r.attend()
        r.Dp(1)
        r.A(2)
        r.C(3)
        r.xrecv(1,"m")
        r.xrecv(1,"n")
        r.query_blocks(["m", "e", "n", "pm", "pe", "pn"])
        r.xrecv(1,"f")
        r.query_blocks(["f", "pf"])
        r.C(2)
        r.Be(2)
        r.Be(3)
        r.Df(2)
        r.section_blocks(["m", "e", "n", "pm", "pe", "pn", "f", "pf"])
        r.Bp(2)
        r.Df(3)
        r.xrecv(2,"m")
        r.xrecv(3,"m")
        r.encode(["m", "e", "n", "pm"])
        r.Dp(2)
        r.Bp(3)
        r.reduce_cores(["m", "e", "n", "pm"])
        r.encode(["f"])
        r.reduce_cores(["f"])
        r.xrecv(2,"n")
        r.xrecv(3,"n")
        r.encode(["pe", "pn"])
        r.Dp(3)
        r.reduce_cores(["pe", "pn"])
        r.xrecv(2,"f")
        r.xrecv(3,"f")
        r.encode(["pf"])
        r.reduce_cores(["pf"])
        r.reduce_heads(["m", "e", "n", "pm"])
        r.reduce_heads(["f"])
        r.reduce_heads(["pe", "pn"])
        r.reduce_heads(["pf"])
        r.place()
        r.finish()

    def end_upper():
        r = Role(True, 1)
        r.A(0)
        r.Bp(0)
        r.Cm(0)
        r.A(1)
        r.xrecv(0,"m")
        r.out_blocks(["e", "pe", "m", "pm"])
        r.C(0)
        r.Bp(1)
        r.Cm(1)
        r.A(2)
        r.A(3)
        r.Df(0)
        pl.semaphore_signal(gate, inc=1, device_id=core, device_id_type=mesh_id)
        r.xrecv(0,"n")
        r.out_blocks(["n", "pn", "f"])
        r.Dp(0)
        r.xrecv(0,"f")
        r.out_blocks(["pf"])
        for c in in_loads:
            c.wait()
        r.attend()
        r.C(1)
        r.send(kg, kg_in, ks.at[0], kr.at[0], mid_peer)
        r.send(vg, vg_in, ks.at[1], kr.at[1], mid_peer)
        r.xrecv(1,"m")
        r.query_blocks(["e", "pe", "m", "pm"])
        r.Df(1)
        r.Dp(1)
        r.xrecv(1,"n")
        r.query_blocks(["n", "pn", "f"])
        r.section_blocks(["e", "pe", "m", "pm"])
        r.xrecv(1,"f")
        r.query_blocks(["pf"])
        r.section_blocks(["n", "pn", "f"])
        r.section_blocks(["pf"])
        r.reduce_cores(["e", "pe", "m", "pm"])
        r.reduce_cores(["n", "pn"])
        r.reduce_cores(["f"])
        r.reduce_heads(["e", "pe", "m", "pm"])
        r.reduce_heads(["n", "pn"])
        r.reduce_cores(["pf"])
        r.reduce_heads(["f"])
        r.reduce_heads(["pf"])
        r.place()
        r.finish()

    def end_lower():
        r = Role(True, 0)
        pl.semaphore_wait(gate, 1)
        r.A(0)
        r.A(1)
        r.Cm(0)
        r.C(0)
        r.Bp(0)
        r.Bp(1)
        r.Df(0)
        r.Cm(1)
        r.xrecv(0,"m")
        r.xrecv(0,"n")
        r.out_blocks(["e", "pe", "m", "pm", "n", "pn"])
        r.C(1)
        r.Df(1)
        r.A(2)
        r.A(3)
        r.Cm(3)
        r.Dp(0)
        r.xrecv(0,"f")
        r.out_blocks(["f", "pf"])
        for c in in_loads:
            c.wait()
        r.attend()
        r.Cm(2)
        r.Bp(2)
        r.Dp(1)
        r.xrecv(1,"m")
        r.xrecv(1,"n")
        r.query_blocks(["e", "pe", "m", "pm", "n", "pn"])
        r.Bp(3)
        r.C(3)
        r.xrecv(1,"f")
        r.query_blocks(["f", "pf"])
        r.C(2)
        r.xrecv(2,"m")
        r.xrecv(3,"m")
        r.encode(["e", "pe", "m", "pm"])
        r.Df(2)
        r.reduce_cores(["e", "pe", "m", "pm"])
        r.section_blocks(["e", "pe", "m", "pm", "n", "pn", "f", "pf"])
        r.Df(3)
        r.xrecv(2,"n")
        r.xrecv(3,"n")
        r.encode(["n", "pn"])
        r.reduce_cores(["n", "pn"])
        r.encode(["f"])
        r.reduce_cores(["f"])
        r.xrecv(2,"f")
        r.xrecv(3,"f")
        r.encode(["pf"])
        r.reduce_cores(["pf"])
        r.reduce_heads(["e", "pe", "m", "pm"])
        r.reduce_heads(["n", "pn"])
        r.reduce_heads(["f"])
        r.reduce_heads(["pf"])
        r.place()
        r.finish()

    for wanted_end, layer, program in (
        (False, 1, mid_upper), (False, 0, mid_lower), (True, 1, end_upper), (True, 0, end_lower)
    ):
        place_here = at_end if wanted_end else jnp.logical_not(at_end)
        pl.when(place_here & (seg == layer))(program)


def run_chain(scalars, owners, top, q, k, v, wo, wq, wk, wv, devices):
    micro = scalars.shape[0]
    q_rows, k_rows = top.shape[0] // micro, k.shape[1] // micro
    width, depth = top.shape[1], q.shape[2]
    half, blocks = width // 2, width // BLOCK
    keys = micro * k_rows
    tiles = keys // TILE
    smem, vmem, any_ = (pl.BlockSpec(memory_space=m) for m in (pltpu.SMEM, pltpu.VMEM, pl.ANY))
    dma = pltpu.SemaphoreType.DMA

    def buf(*shape, dtype=BF16):
        return pltpu.VMEM(shape, dtype)

    return pl.pallas_call(
        functools.partial(chain_kernel, (q_rows, k_rows, depth // DH, devices)),
        in_specs=[smem, smem] + [any_] * 8,
        out_specs=[vmem, vmem],
        out_shape=[
            jax.ShapeDtypeStruct((1, micro * q_rows, half), BF16),
            jax.ShapeDtypeStruct((keys, width // 4), BF16),
        ],
        scratch_shapes=[
            buf(4, blocks, depth, BLOCK),
            buf(blocks, micro * q_rows, BLOCK),
            buf(micro * q_rows, depth),
            buf(keys, depth),
            buf(keys, depth),
            buf(micro * q_rows, depth, dtype=F32),
            buf(micro * q_rows, depth),
            buf(keys, depth),
            buf(keys, depth),
            buf(blocks, micro * q_rows, BLOCK),
            buf(blocks, micro * q_rows, BLOCK),
            buf(blocks, keys, BLOCK),
            buf(4, keys, BLOCK),
            buf(2, keys, BLOCK),
            buf(2, keys, BLOCK),
            buf(keys, depth),
            buf(keys, depth),
            buf(blocks, keys, BLOCK),
            buf(4, keys, BLOCK),
            buf(2, keys, BLOCK),
            buf(2, tiles, TILE, BLOCK),
            buf(2, 2 * CAP, TILE, BLOCK),
            buf(2, 2 * CAP, TILE, BLOCK),
        ]
        + [dma((4,)), dma((8,)), dma((3,))]
        + [dma((9, 4))] * 2
        + [dma((4, 4))] * 2
        + [dma((8,))] * 4
        + [dma((2,))] * 2
        + [dma((8,))] * 2
        + [dma((2,))] * 2
        + [dma((4,))] * 2
        + [dma((4,)), dma((2,))]
        + [dma((2, 2))] * 2
        + [pltpu.SemaphoreType.REGULAR],
        compiler_params=pltpu.CompilerParams(
            collective_id=0, has_side_effects=True, vmem_limit_bytes=60 << 20
        ),
    )(scalars, owners, top, q, k, v, wo, wq, wk, wv)


def ranked(marked):
    ids = jnp.arange(marked.shape[0], dtype=jnp.int32)
    upto = ids[None, :] <= ids[:, None]
    return jnp.sum((upto & marked[None, :]).astype(jnp.int32), axis=1) - 1


def on_device(
    grad_top,
    saved_query,
    saved_key,
    saved_value,
    w_query,
    w_key,
    w_value,
    w_out,
    query_length,
    key_offset,
    key_length,
    tile_owner,
):
    seg = lax.axis_index("segment")
    mp = lax.axis_index("mp")
    devices = lax.axis_size("dp")
    me = lax.axis_index("dp")
    micro = query_length.shape[0]
    q_rows = grad_top.shape[0] // micro
    k_rows = saved_key.shape[1] // micro
    half = grad_top.shape[1] // 2
    mp_swap = [(0, 1), (1, 0)]
    if w_out.shape[2] == BLOCK and devices == 8 and micro == 2:
        table = jnp.concatenate([query_length, key_offset, key_length], axis=1)
        return run_chain(
            table, tile_owner, grad_top, saved_query, saved_key, saved_value, w_out, w_query, w_key,
            w_value, devices,
        )

    wo, sources = gathered(w_out[0])
    wq, _ = gathered(w_query[0])
    wk, _ = gathered(w_key[0])
    wv, _ = gathered(w_value[0])
    order = jnp.stack(sources).astype(jnp.int32)

    top = grad_top.reshape(grad_top.shape[0], 2, half).transpose(1, 0, 2)
    scalars = [
        jnp.concatenate([order, query_length[s], key_offset[s], key_length[s]])
        for s in range(micro)
    ]

    def tick(s, grad, at):
        return run_tick(
            scalars[s], grad, at, s, saved_query, saved_key, saved_value, wo, wq, q_rows, k_rows
        )

    upper = [tick(s, top, s) for s in range(micro)]
    upper_half, incoming = [], []
    for s in range(micro):
        mixed = upper[s][0]
        other = lax.ppermute(mixed, "mp", mp_swap)
        rows = top[:, s * q_rows : (s + 1) * q_rows]
        section = (rows.astype(F32) + (mixed.astype(F32) + other.astype(F32))).astype(BF16)
        incoming.append(lax.ppermute(section, "segment", [(1, 0)]))
        upper_half.append(lax.dynamic_index_in_dim(section, mp, 0, keepdims=False))
    lower = [tick(s, incoming[s], 0) for s in range(micro)]
    halves = []
    for s in range(micro):
        mixed = lower[s][0]
        other = lax.ppermute(
            lax.dynamic_index_in_dim(mixed, 1 - mp, 0, keepdims=False), "mp", mp_swap
        )
        own = lax.dynamic_index_in_dim(mixed, mp, 0, keepdims=False)
        base = lax.dynamic_index_in_dim(incoming[s], mp, 0, keepdims=False)
        low = (base.astype(F32) + (own.astype(F32) + other.astype(F32))).astype(BF16)
        halves.append(jnp.where(seg == 1, upper_half[s], low))
    sections = jnp.concatenate(halves, axis=0)[None]

    kg = jnp.concatenate([jnp.where(seg == 1, upper[s][1], lower[s][1]) for s in range(micro)], 0)
    vg = jnp.concatenate([jnp.where(seg == 1, upper[s][2], lower[s][2]) for s in range(micro)], 0)
    parts = run_encoder(order, kg, vg, wk, wv)
    away = lax.dynamic_slice_in_dim(parts, (1 - seg) * 2, 2, 0)
    mine = lax.dynamic_slice_in_dim(parts, seg * 2, 2, 0)
    arrived = lax.ppermute(away, "segment", mp_swap)
    summed = (mine.astype(F32) + arrived.astype(F32)).astype(BF16)
    crossing = lax.ppermute(
        lax.dynamic_index_in_dim(summed, 1 - mp, 0, keepdims=False), "mp", mp_swap
    )
    kept = lax.dynamic_index_in_dim(summed, mp, 0, keepdims=False)
    kept = (kept.astype(F32) + crossing.astype(F32)).astype(BF16)

    tiles = kept.shape[0] // TILE
    features = kept.shape[1]
    owners = tile_owner.reshape(devices, tiles)
    slot_ids = jnp.arange(CAP, dtype=jnp.int32)[:, None]
    tile_ids = jnp.arange(tiles, dtype=jnp.int32)

    def plan(source):
        source = source % devices
        row = lax.dynamic_index_in_dim(owners, source, 0, keepdims=False)
        return (row // tiles - source + devices) % devices, row % tiles

    def ranks_of(marked):
        return (ranked(marked)[None, :] == slot_ids) & marked[None, :]

    step, slot = plan(me)
    left_step, left_slot = plan(me - 1 + devices)
    right_step, right_slot = plan(me + 1)
    send_left = jnp.sum(jnp.where(ranks_of(step == devices - 1), tile_ids[None, :], 0), axis=1)
    send_right = jnp.sum(jnp.where(ranks_of(step == 1), tile_ids[None, :], 0), axis=1)
    left_hit = ranks_of(left_step == 1)
    right_hit = ranks_of(right_step == devices - 1)
    target = jnp.concatenate(
        [
            jnp.sum(jnp.where(left_hit, left_slot[None, :], 0), axis=1),
            slot,
            jnp.sum(jnp.where(right_hit, right_slot[None, :], 0), axis=1),
        ]
    )
    usable = jnp.concatenate([jnp.any(left_hit, axis=1), step == 0, jnp.any(right_hit, axis=1)])
    chosen = (tile_ids[:, None] == target[None, :]) & usable[None, :]
    candidate_ids = jnp.arange(target.shape[0], dtype=jnp.int32)
    take = jnp.sum(jnp.where(chosen, candidate_ids[None, :], 0), axis=1)

    tiled = (tiles, TILE, features)
    shape = jax.ShapeDtypeStruct(tiled, BF16)
    handed = jax.ShapeDtypeStruct((CAP, TILE, features), BF16)
    local = kept.reshape(tiled)
    to_left, to_right = small_call(
        pick_kernel, jnp.concatenate([send_left, send_right]), [local], [handed, handed]
    )
    forward = [(i, (i + 1) % devices) for i in range(devices)]
    backward = [(b, a) for a, b in forward]
    from_left = lax.ppermute(to_right, "dp", forward)
    from_right = lax.ppermute(to_left, "dp", backward)
    owned = small_call(place_kernel, take, [from_left, local, from_right], shape)
    return sections, owned.reshape(tiles * TILE, features)


def solution(mesh):
    in_specs = (
        P("dp", None),
        P("segment", "dp", "mp"),
        P("segment", "dp", "mp"),
        P("segment", "dp", "mp"),
        P("segment", "mp", "dp"),
        P("segment", "mp", "dp"),
        P("segment", "mp", "dp"),
        P("segment", "mp", "dp"),
        P("dp", None),
        P("dp", None),
        P("dp", None),
        P(),
    )
    out_specs = (P("segment", "dp", "mp"), P("dp", ("segment", "mp")))
    return jax.shard_map(
        on_device, mesh=mesh, in_specs=in_specs, out_specs=out_specs, check_vma=False
    )
```

profile of v0, /device:TPU:0, one launch (start us, length us, event | category | flops | bytes accessed | tf_op | source)
XLA Modules:
  0.0 175.3 jit_solution(15303960274102971355)
XLA Ops:
  0.6 1.3 pad_add_fusion.sc
  2.0 1.4 copy.14.own
  3.3 168.7 %shard_map.131 = (bf16[1,512,1024]{2,1,0:T(8,128)(2,1)}, bf16[768,512]{1,0:T(8,128)(2,1)}) custom-call(s32[2,6]{1,0:T(2,128)} %pad_add_fusion.sc, s32[16,3]{1,0:T(8,128)} %copy.14.own, bf16[512,2048]{1,0:T(8,128)(2,1)} %top_hbm.1, bf16[1,512,1024]{2,1,0:T(8,128)(2,1)} %q_hbm.1, bf16[1,768,1024]{2,1,0:T(8,128)(2,1)} %k_hbm.1, bf16[1,768,1024]{2,1,0:T(8,128)(2,1)} %v_hbm.1, ...), custom_call_target="tpu_custom_call" | custom-call | tf_op jit(solution)/shard_map/pallas_call | solution.py:961
  172.1 0.0 copy-start
  172.1 2.3 %copy.17 = bf16[1,512,1024]{2,1,0:T(8,128)(2,1)} copy(bf16[1,512,1024]{2,1,0:T(8,128)(2,1)} %get-tuple-element.4) | data formatting | bytes 2097152
  174.4 0.0 copy-done
  174.4 0.9 copy.18
Async XLA Ops:
  172.1 2.3 %copy-start = (bf16[768,512]{1,0:T(8,128)(2,1)S(1)}, bf16[768,512]{1,0:T(8,128)(2,1)}, u32[]{:S(2)}) copy-start(bf16[768,512]{1,0:T(8,128)(2,1)} %get-tuple-element.5) | copy-start | bytes 2359300
where the time goes:
time: 177 us; the launch traced here: 175 us
  Pallas kernels  169 us (95%)
  local copies, waits for them, and re-layouts  4.57 us (3%)
    pallas_call x1, Pallas kernels, run_chain(): pl.pallas_call(functools.partial(chain_kernel, (q_rows, k_rows, depth //...  169 us
    unnamed x5, local copies, waits for them, and re-layouts  4.57 us

commit v1 on v0

--- a/solution.py
+++ b/solution.py
@@ -184,12 +184,13 @@
     return blocks, list(jnp.arange(len(blocks), dtype=jnp.int32))
 
 
-def chain_kernel(dims, sc, own, top_hbm, q_hbm, k_hbm, v_hbm, wo_hbm, wq_hbm, wk_hbm, wv_hbm,
-                 sections_ref, out_ref,
+def chain_kernel(dims, ql_hbm, ko_hbm, kl_hbm, own_hbm, top_hbm, q_hbm, k_hbm, v_hbm, wo_hbm, wq_hbm, wk_hbm, wv_hbm,
+                 sections_hbm, out_ref,
                  wbuf, g, q_ref, k_ref, v_ref, acc, qg, kg, vg, mixed, other, parts, near, fwd, far,
                  kg_in, vg_in, lent, lent_in, back, loc, inc, snd,
                  ldw, ldg, ldq, zs, zr, xs, xr, ms, mr, gs, gr, ks, kr, ps, pr, ys, yr,
-                 us, ur, rs, rr, hs, hr, gate):
+                 us, ur, rs, rr, hs, hr, so, gate,
+                 q_len_of, k_off_of, k_len_of, own, ldt):
     q_rows, k_rows, heads, devices = dims
     depth = heads * DH
     scale = DH ** (-0.5)
@@ -221,6 +222,8 @@
         cols = pl.ds(pl.multiple_of(b * BLOCK, BLOCK), BLOCK)
         return load(top_hbm.at[:, cols], g.at[b], ldg.at[b])
 
+    tables = ((ql_hbm, q_len_of), (ko_hbm, k_off_of), (kl_hbm, k_len_of), (own_hbm, own))
+    table_loads = [load(a, b, ldt.at[i]) for i, (a, b) in enumerate(tables)]
     w_loads[0].start()
 
     barrier = pltpu.get_barrier_semaphore()
@@ -253,7 +256,7 @@
         for b in range(8):
             g_load(b).start()
 
-    for c in w_loads[1:] + in_loads:
+    for c in w_loads[1:] + in_loads + table_loads:
         c.start()
     for c in w_loads:
         c.wait()
@@ -332,6 +335,8 @@
                 return carry
 
             lax.fori_loop(0, 8, one, 0)
+            for i in range(4):
+                self.output_copy(4 * mp + i).wait()
 
         def start(self, make, b):
             copy, cond = make(b)
@@ -353,12 +358,13 @@
         def lent_unit(self, u):
             return self.layer == 1 and u >= 2
 
+        def twice(self, u):
+            return u < (2 if self.layer == 1 else 1)
+
         def x_rows(self, u, name):
             if name != "f":
                 return whole
-            if self.end:
-                return lower if u < 2 else whole
-            return whole if self.lent_unit(u) else lower
+            return lower if not self.end or self.twice(u) else whole
 
         def xsend(self, u, name):
             ref = self.w(u, name, self.x_rows(u, name))
@@ -390,8 +396,11 @@
             if self.end:
                 self.xrecv(u, "e")
                 self.zsend(1, u, "pe", mid_peer)
-            elif not self.lent_unit(u):
-                self.zrecv(1, u, "pe")
+            else:
+                if self.lent_unit(u):
+                    self.xrecv(u, "e")
+                else:
+                    self.zrecv(1, u, "pe")
                 self.zsend(8, u, "pe", far_mid, upper)
 
         def Cm(self, u):
@@ -419,11 +428,10 @@
 
         def Dp(self, u):
             if self.end:
-                if u < 2:
-                    self.zrecv(5, u, "pf", upper)
-            elif not self.lent_unit(u):
+                self.zrecv(5, u, "pf", upper)
+            else:
                 self.zrecv(8, u, "pf", upper)
-                if u < 2:
+                if self.twice(u):
                     self.zsend(5, u, "pf", end_peer, upper)
 
 
@@ -472,6 +480,11 @@
             return (self.remote(snd.at[j, pl.ds(CAP, CAP)], inc.at[j, pl.ds(0, CAP)], hs.at[j, 1],
                                 hr.at[j, 1], (seg, (me + 1) % devices, mp)), self.mine(b))
 
+        def output_copy(self, b):
+            cols = pl.ds(pl.multiple_of((b % 4) * BLOCK, BLOCK), BLOCK)
+            src = g.at[b] if self.layer == 1 else mixed.at[b]
+            return load(src, sections_hbm.at[0, :, cols], so.at[b % 4])
+
 
         def out_blocks(self, names):
             if not self.started:
@@ -500,7 +513,7 @@
                 kr_ = pl.ds(pl.multiple_of(s * k_rows, k_rows), k_rows)
                 allowed = None
                 for e in range(2):
-                    q_len, k_off, k_len = sc[s, e], sc[s, 2 + e] * TILE, sc[s, 4 + e]
+                    q_len, k_off, k_len = q_len_of[s, e], k_off_of[s, e] * TILE, k_len_of[s, e]
                     hit = (rows >= e * TILE) & (rows < e * TILE + q_len)
                     hit = hit & (cols >= k_off) & (cols < k_off + k_len)
                     allowed = hit if allowed is None else allowed | hit
@@ -542,7 +555,6 @@
                 return (g[b, rows, :].astype(F32) + change).astype(BF16)
 
             def block(b):
-                cols = pl.ds(pl.multiple_of((b % 4) * BLOCK, BLOCK), BLOCK)
                 if self.layer == 1:
                     self.recv(other.at[b], ms.at[b], mr.at[b])
 
@@ -551,18 +563,20 @@
 
                     loop(2 * q_rows, body)
                     self.start(self.section_copy, b)
+                else:
+
+                    @pl.when(b // 4 == mp)
+                    def _():
+                        self.recv(other.at[b], ms.at[b], mr.at[b])
+
+                        def body(rows):
+                            mixed[b, rows, :] = total(b, rows)
+
+                        loop(2 * q_rows, body)
 
                 @pl.when(b // 4 == mp)
                 def _():
-                    if self.layer == 0:
-                        self.recv(other.at[b], ms.at[b], mr.at[b])
-
-                    def body(rows):
-                        sections_ref[0, rows, cols] = (
-                            g[b, rows, :] if self.layer == 1 else total(b, rows)
-                        )
-
-                    loop(2 * q_rows, body)
+                    self.output_copy(b).start()
 
             each(names, block)
 
@@ -672,11 +686,15 @@
                         i < tiles, kept, came
                     )
 
+    for c in table_loads:
+        c.wait()
+
     tiles = 2 * k_rows // TILE
+
     per = tiles // 2
 
     def globals_of(source):
-        return [own[source * 2 + t // per, t % per] for t in range(tiles)]
+        return [own[t % per, source * 2 + t // per] for t in range(tiles)]
 
     def picks(goes, to):
         seen, chosen = jnp.int32(0), [jnp.int32(0)] * CAP
@@ -705,66 +723,70 @@
         r.A(0)
         r.Be(0)
         r.C(0)
-        pl.semaphore_signal(gate, inc=1, device_id=core, device_id_type=mesh_id)
-        r.xrecv(0,"m")
-        r.out_blocks(["m", "e", "n", "pm"])
-        r.Bp(0)
         r.A(1)
         r.Df(0)
+        r.Bp(0)
+        r.xrecv(0,"m")
         r.xrecv(0,"n")
-        r.out_blocks(["pe", "pn", "f"])
+        r.out_blocks(["m", "e", "n", "f", "pm", "pe", "pn"])
         r.Be(1)
+        r.C(1)
         r.Dp(0)
-        r.C(1)
-        r.Bp(1)
+        pl.semaphore_signal(gate, inc=1, device_id=core, device_id_type=mesh_id)
         r.xrecv(0,"f")
         r.out_blocks(["pf"])
         for c in in_loads:
             c.wait()
         r.attend()
         r.Df(1)
-        r.Dp(1)
+        r.Bp(1)
         r.A(2)
         r.A(3)
         r.Be(2)
-        r.Be(3)
+        r.query_blocks(["m", "e", "n"])
         r.xrecv(1,"m")
-        r.query_blocks(["m", "e", "n", "pm"])
+        r.query_blocks(["f", "pm", "pe"])
         r.xrecv(1,"n")
-        r.query_blocks(["pe", "pn", "f"])
+        r.query_blocks(["pn"])
+        r.Dp(1)
         r.xrecv(1,"f")
         r.query_blocks(["pf"])
+        r.Be(3)
+        r.section_blocks(["m", "e", "n"])
         r.C(2)
+        r.section_blocks(["f", "pm", "pe"])
+        r.section_blocks(["pn"])
+        r.section_blocks(["pf"])
         r.C(3)
-        r.section_blocks(["m", "e", "n", "pm"])
+        r.Bp(2)
         r.Df(2)
-        r.section_blocks(["pe", "pn", "f"])
-        r.section_blocks(["pf"])
         r.Df(3)
+        r.encode(["m", "e", "n", "f"])
+        r.Dp(2)
+        r.Bp(3)
         r.xrecv(2,"m")
         r.xrecv(3,"m")
-        r.xrecv(2,"e")
-        r.xrecv(3,"e")
+        r.encode(["pm", "pe"])
+        r.Dp(3)
+        r.recv(kg_in, ks.at[0], kr.at[0])
+        r.recv(vg_in, ks.at[1], kr.at[1])
+        r.encode_lent(["m", "e", "n", "f"])
+        r.encode_lent(["pm", "pe"])
         r.xrecv(2,"n")
         r.xrecv(3,"n")
-        r.encode(["m", "e", "n", "pm", "pe", "pn"])
-        r.recv(kg_in, ks.at[0], kr.at[0])
-        r.recv(vg_in, ks.at[1], kr.at[1])
-        r.encode_lent(["m", "e", "n", "pm", "pe", "pn"])
         r.xrecv(2,"f")
         r.xrecv(3,"f")
-        r.encode(["f", "pf"])
-        r.encode_lent(["f", "pf"])
-        r.give_back(["m", "e", "n", "pm", "pe", "pn"])
-        r.reduce_cores(["m", "e", "n", "pm"])
-        r.reduce_cores(["f"])
-        r.give_back(["f", "pf"])
-        r.reduce_cores(["pe", "pn"])
-        r.reduce_cores(["pf"])
-        r.reduce_heads(["m", "e", "n", "pm"])
-        r.reduce_heads(["f"])
-        r.reduce_heads(["pe", "pn"])
-        r.reduce_heads(["pf"])
+        r.encode(["pn", "pf"])
+        r.encode_lent(["pn", "pf"])
+        r.give_back(["m", "e", "n", "f"])
+        r.give_back(["pm", "pe"])
+        r.reduce_cores(["m", "e", "n", "f"])
+        r.give_back(["pn", "pf"])
+        r.reduce_cores(["pm", "pe"])
+        r.reduce_cores(["pn", "pf"])
+        r.reduce_heads(["m", "e", "n", "f"])
+        r.reduce_heads(["pm", "pe"])
+        r.reduce_heads(["pn", "pf"])
         r.place()
         r.finish()
 
@@ -772,61 +794,60 @@
         r = Role(False, 0)
         pl.semaphore_wait(gate, 1)
         r.A(0)
+        r.A(1)
         r.C(0)
         r.Be(0)
+        r.C(1)
+        r.Be(1)
+        r.out_blocks(["m", "e", "n"])
+        r.Bp(0)
         r.Df(0)
-        r.A(1)
-        r.Be(1)
-        r.Bp(0)
         r.xrecv(0,"m")
+        r.out_blocks(["f", "pm", "pe"])
         r.xrecv(0,"n")
-        r.out_blocks(["m", "e", "n", "pm", "pe", "pn"])
+        r.out_blocks(["pn"])
         r.Bp(1)
-        r.C(1)
         r.Df(1)
-        r.A(3)
         r.Dp(0)
         r.xrecv(0,"f")
-        r.out_blocks(["f", "pf"])
+        r.out_blocks(["pf"])
         for c in in_loads:
             c.wait()
         r.attend()
         r.Dp(1)
         r.A(2)
-        r.C(3)
         r.xrecv(1,"m")
         r.xrecv(1,"n")
-        r.query_blocks(["m", "e", "n", "pm", "pe", "pn"])
+        r.query_blocks(["m", "e", "n", "f", "pm", "pe", "pn"])
         r.xrecv(1,"f")
-        r.query_blocks(["f", "pf"])
+        r.query_blocks(["pf"])
+        r.Be(2)
         r.C(2)
-        r.Be(2)
+        r.A(3)
+        r.Df(2)
+        r.section_blocks(["m", "e", "n", "f", "pm", "pe", "pn", "pf"])
         r.Be(3)
-        r.Df(2)
-        r.section_blocks(["m", "e", "n", "pm", "pe", "pn", "f", "pf"])
+        r.C(3)
         r.Bp(2)
         r.Df(3)
+        r.encode(["m", "e", "n", "f"])
+        r.Dp(2)
+        r.Bp(3)
+        r.reduce_cores(["m", "e", "n", "f"])
         r.xrecv(2,"m")
         r.xrecv(3,"m")
-        r.encode(["m", "e", "n", "pm"])
-        r.Dp(2)
-        r.Bp(3)
-        r.reduce_cores(["m", "e", "n", "pm"])
-        r.encode(["f"])
-        r.reduce_cores(["f"])
+        r.encode(["pm", "pe"])
+        r.reduce_cores(["pm", "pe"])
+        r.Dp(3)
         r.xrecv(2,"n")
         r.xrecv(3,"n")
-        r.encode(["pe", "pn"])
-        r.Dp(3)
-        r.reduce_cores(["pe", "pn"])
         r.xrecv(2,"f")
         r.xrecv(3,"f")
-        r.encode(["pf"])
-        r.reduce_cores(["pf"])
-        r.reduce_heads(["m", "e", "n", "pm"])
-        r.reduce_heads(["f"])
-        r.reduce_heads(["pe", "pn"])
-        r.reduce_heads(["pf"])
+        r.encode(["pn", "pf"])
+        r.reduce_cores(["pn", "pf"])
+        r.reduce_heads(["m", "e", "n", "f"])
+        r.reduce_heads(["pm", "pe"])
+        r.reduce_heads(["pn", "pf"])
         r.place()
         r.finish()
 
@@ -834,10 +855,8 @@
         r = Role(True, 1)
         r.A(0)
         r.Bp(0)
+        r.A(1)
         r.Cm(0)
-        r.A(1)
-        r.xrecv(0,"m")
-        r.out_blocks(["e", "pe", "m", "pm"])
         r.C(0)
         r.Bp(1)
         r.Cm(1)
@@ -845,35 +864,34 @@
         r.A(3)
         r.Df(0)
         pl.semaphore_signal(gate, inc=1, device_id=core, device_id_type=mesh_id)
+        r.xrecv(0,"m")
         r.xrecv(0,"n")
-        r.out_blocks(["n", "pn", "f"])
+        r.out_blocks(["e", "pe", "m", "pm", "n", "pn", "f"])
+        r.C(1)
         r.Dp(0)
         r.xrecv(0,"f")
         r.out_blocks(["pf"])
         for c in in_loads:
             c.wait()
         r.attend()
-        r.C(1)
         r.send(kg, kg_in, ks.at[0], kr.at[0], mid_peer)
         r.send(vg, vg_in, ks.at[1], kr.at[1], mid_peer)
         r.xrecv(1,"m")
-        r.query_blocks(["e", "pe", "m", "pm"])
+        r.xrecv(1,"n")
+        r.query_blocks(["e", "pe", "m", "pm", "n", "pn"])
         r.Df(1)
         r.Dp(1)
-        r.xrecv(1,"n")
-        r.query_blocks(["n", "pn", "f"])
-        r.section_blocks(["e", "pe", "m", "pm"])
         r.xrecv(1,"f")
-        r.query_blocks(["pf"])
-        r.section_blocks(["n", "pn", "f"])
-        r.section_blocks(["pf"])
-        r.reduce_cores(["e", "pe", "m", "pm"])
-        r.reduce_cores(["n", "pn"])
-        r.reduce_cores(["f"])
-        r.reduce_heads(["e", "pe", "m", "pm"])
-        r.reduce_heads(["n", "pn"])
+        r.query_blocks(["f", "pf"])
+        r.section_blocks(["e", "pe", "m", "pm", "n", "pn"])
+        r.section_blocks(["f", "pf"])
+        r.reduce_cores(["e", "pe", "m"])
+        r.reduce_cores(["pm", "n"])
+        r.reduce_heads(["pm", "n"])
+        r.reduce_heads(["e", "pe", "m"])
+        r.reduce_cores(["pn", "f"])
         r.reduce_cores(["pf"])
-        r.reduce_heads(["f"])
+        r.reduce_heads(["pn", "f"])
         r.reduce_heads(["pf"])
         r.place()
         r.finish()
@@ -884,56 +902,56 @@
         r.A(0)
         r.A(1)
         r.Cm(0)
+        r.Bp(0)
+        r.Cm(1)
+        r.Bp(1)
         r.C(0)
-        r.Bp(0)
-        r.Bp(1)
+        r.C(1)
         r.Df(0)
-        r.Cm(1)
-        r.xrecv(0,"m")
-        r.xrecv(0,"n")
-        r.out_blocks(["e", "pe", "m", "pm", "n", "pn"])
-        r.C(1)
         r.Df(1)
         r.A(2)
-        r.A(3)
-        r.Cm(3)
         r.Dp(0)
+        r.xrecv(0,"m")
+        r.out_blocks(["e", "pe", "m", "pm"])
+        r.xrecv(0,"n")
         r.xrecv(0,"f")
-        r.out_blocks(["f", "pf"])
+        r.out_blocks(["n", "pn", "f", "pf"])
         for c in in_loads:
             c.wait()
         r.attend()
         r.Cm(2)
+        r.A(3)
         r.Bp(2)
-        r.Dp(1)
         r.xrecv(1,"m")
+        r.query_blocks(["e", "pe", "m", "pm"])
         r.xrecv(1,"n")
-        r.query_blocks(["e", "pe", "m", "pm", "n", "pn"])
-        r.Bp(3)
-        r.C(3)
+        r.query_blocks(["n", "pn"])
         r.xrecv(1,"f")
         r.query_blocks(["f", "pf"])
         r.C(2)
+        r.Cm(3)
+        r.Bp(3)
+        r.encode(["e", "pe", "m"])
+        r.Df(2)
+        r.reduce_cores(["e", "pe", "m"])
+        r.section_blocks(["e", "pe", "m", "pm", "n", "pn", "f", "pf"])
+        r.C(3)
         r.xrecv(2,"m")
         r.xrecv(3,"m")
-        r.encode(["e", "pe", "m", "pm"])
-        r.Df(2)
-        r.reduce_cores(["e", "pe", "m", "pm"])
-        r.section_blocks(["e", "pe", "m", "pm", "n", "pn", "f", "pf"])
+        r.encode(["pm", "n"])
         r.Df(3)
+        r.reduce_cores(["pm", "n"])
         r.xrecv(2,"n")
         r.xrecv(3,"n")
-        r.encode(["n", "pn"])
-        r.reduce_cores(["n", "pn"])
-        r.encode(["f"])
-        r.reduce_cores(["f"])
+        r.encode(["pn", "f"])
+        r.reduce_cores(["pn", "f"])
+        r.reduce_heads(["pm", "n"])
         r.xrecv(2,"f")
         r.xrecv(3,"f")
         r.encode(["pf"])
         r.reduce_cores(["pf"])
-        r.reduce_heads(["e", "pe", "m", "pm"])
-        r.reduce_heads(["n", "pn"])
-        r.reduce_heads(["f"])
+        r.reduce_heads(["e", "pe", "m"])
+        r.reduce_heads(["pn", "f"])
         r.reduce_heads(["pf"])
         r.place()
         r.finish()
@@ -945,23 +963,23 @@
         pl.when(place_here & (seg == layer))(program)
 
 
-def run_chain(scalars, owners, top, q, k, v, wo, wq, wk, wv, devices):
-    micro = scalars.shape[0]
+def run_chain(tables, top, q, k, v, wo, wq, wk, wv, devices):
+    micro = tables[0].shape[0]
     q_rows, k_rows = top.shape[0] // micro, k.shape[1] // micro
     width, depth = top.shape[1], q.shape[2]
     half, blocks = width // 2, width // BLOCK
     keys = micro * k_rows
     tiles = keys // TILE
-    smem, vmem, any_ = (pl.BlockSpec(memory_space=m) for m in (pltpu.SMEM, pltpu.VMEM, pl.ANY))
+    vmem, any_ = (pl.BlockSpec(memory_space=m) for m in (pltpu.VMEM, pl.ANY))
     dma = pltpu.SemaphoreType.DMA
 
     def buf(*shape, dtype=BF16):
         return pltpu.VMEM(shape, dtype)
 
-    return pl.pallas_call(
+    sections, owned = pl.pallas_call(
         functools.partial(chain_kernel, (q_rows, k_rows, depth // DH, devices)),
-        in_specs=[smem, smem] + [any_] * 8,
-        out_specs=[vmem, vmem],
+        in_specs=[any_] * 12,
+        out_specs=[any_, vmem],
         out_shape=[
             jax.ShapeDtypeStruct((1, micro * q_rows, half), BF16),
             jax.ShapeDtypeStruct((keys, width // 4), BF16),
@@ -1001,11 +1019,40 @@
         + [dma((4,))] * 2
         + [dma((4,)), dma((2,))]
         + [dma((2, 2))] * 2
-        + [pltpu.SemaphoreType.REGULAR],
+        + [dma((4,))]
+        + [pltpu.SemaphoreType.REGULAR]
+        + [pltpu.SMEM(t.shape, jnp.int32) for t in tables]
+        + [dma((4,))],
         compiler_params=pltpu.CompilerParams(
             collective_id=0, has_side_effects=True, vmem_limit_bytes=60 << 20
         ),
-    )(scalars, owners, top, q, k, v, wo, wq, wk, wv)
+    )(*tables, top, q, k, v, wo, wq, wk, wv)
+    return pl.pallas_call(
+        hand_over_kernel,
+        in_specs=[any_] * 2,
+        out_specs=[any_] * 2,
+        out_shape=[jax.ShapeDtypeStruct(a.shape, a.dtype) for a in (sections, owned)],
+        scratch_shapes=[pltpu.VMEM(a.shape, a.dtype) for a in (sections, owned)] + [dma((2, 2, 4))],
+    )(sections, owned)
+
+
+def hand_over_kernel(a_in, b_in, a_out, b_out, a_mid, b_mid, sems):
+    inward, outward = [], []
+    for i in range(4):
+        for n, (src, mid, dst) in enumerate(
+            ((a_in.at[0], a_mid.at[0], a_out.at[0]), (b_in, b_mid, b_out))
+        ):
+            rows = src.shape[0] // 4
+            at = pl.ds(i * rows, rows)
+            inward.append(pltpu.make_async_copy(src.at[at], mid.at[at], sems.at[0, n, i]))
+            outward.append(pltpu.make_async_copy(mid.at[at], dst.at[at], sems.at[1, n, i]))
+    for c in inward:
+        c.start()
+    for c, d in zip(inward, outward):
+        c.wait()
+        d.start()
+    for d in outward:
+        d.wait()
 
 
 def ranked(marked):
@@ -1038,10 +1085,9 @@
     half = grad_top.shape[1] // 2
     mp_swap = [(0, 1), (1, 0)]
     if w_out.shape[2] == BLOCK and devices == 8 and micro == 2:
-        table = jnp.concatenate([query_length, key_offset, key_length], axis=1)
         return run_chain(
-            table, tile_owner, grad_top, saved_query, saved_key, saved_value, w_out, w_query, w_key,
-            w_value, devices,
+            (query_length, key_offset, key_length, tile_owner.T), grad_top, saved_query, saved_key,
+            saved_value, w_out, w_query, w_key, w_value, devices,
         )
 
     wo, sources = gathered(w_out[0])

time: 177 us -> 163 us (0.921)
  Pallas kernels: 169 us -> 161 us
  local copies, waits for them, and re-layouts: 4.57 us -> 0 us
    pallas_call x1, Pallas kernels: 169 us -> 158 us  [run_chain(): pl.pallas_call(functools.partial(chain_kernel, (q_rows, k_rows, depth //...]
    unnamed x5 -> x0, local copies, waits for them, and re-layouts: 4.57 us -> none
    pallas_call x0 -> x1, Pallas kernels: none -> 2.33 us  [run_chain(): pl.pallas_call(hand_over_kernel, in_specs=[any_] * 2, out_specs=[any_] *...]
where the time goes in v1:
time: 163 us; the launch traced here: 162 us
  Pallas kernels  161 us (99%)
    pallas_call x1, Pallas kernels, run_chain(): pl.pallas_call(functools.partial(chain_kernel, (q_rows, k_rows, depth //...  158 us

profile of v1, /device:TPU:0, one launch (start us, length us, event | category | flops | bytes accessed | tf_op | source)
XLA Modules:
  0.0 161.5 jit_solution(1343872573507904946)
XLA Ops:
  0.6 158.4 %shard_map.131 = (bf16[1,512,1024]{2,1,0:T(8,128)(2,1)}, bf16[768,512]{1,0:T(8,128)(2,1)}) custom-call(s32[2,2]{1,0:T(2,128)} %ql_hbm.1, s32[2,2]{1,0:T(2,128)} %ko_hbm.1, s32[2,2]{1,0:T(2,128)} %kl_hbm.1, s32[3,16]{1,0:T(4,128)} %bitcast.1, bf16[512,2048]{1,0:T(8,128)(2,1)} %top_hbm.1, bf16[1,512,1024]{2,1,0:T(8,128)(2,1)} %q_hbm.1, ...), custom_call_target="tpu_custom_call" | custom-call | tf_op jit(solution)/shard_map/pallas_call | solution.py:979
  159.0 2.3 %shard_map.132 = (bf16[1,512,1024]{2,1,0:T(8,128)(2,1)}, bf16[768,512]{1,0:T(8,128)(2,1)}) custom-call(bf16[1,512,1024]{2,1,0:T(8,128)(2,1)} %get-tuple-element.4.a_in, bf16[768,512]{1,0:T(8,128)(2,1)} %get-tuple-element.5.b_in), custom_call_target="tpu_custom_call" | custom-call | tf_op jit(solution)/shard_map/pallas_call | solution.py:1030

commit v2 on v1

--- a/solution.py
+++ b/solution.py
@@ -741,7 +741,6 @@
         r.Df(1)
         r.Bp(1)
         r.A(2)
-        r.A(3)
         r.Be(2)
         r.query_blocks(["m", "e", "n"])
         r.xrecv(1,"m")
@@ -751,26 +750,27 @@
         r.Dp(1)
         r.xrecv(1,"f")
         r.query_blocks(["pf"])
-        r.Be(3)
         r.section_blocks(["m", "e", "n"])
         r.C(2)
         r.section_blocks(["f", "pm", "pe"])
         r.section_blocks(["pn"])
         r.section_blocks(["pf"])
-        r.C(3)
         r.Bp(2)
         r.Df(2)
+        r.A(3)
+        r.Be(3)
+        r.Dp(2)
+        r.C(3)
         r.Df(3)
         r.encode(["m", "e", "n", "f"])
-        r.Dp(2)
         r.Bp(3)
         r.xrecv(2,"m")
         r.xrecv(3,"m")
         r.encode(["pm", "pe"])
-        r.Dp(3)
         r.recv(kg_in, ks.at[0], kr.at[0])
         r.recv(vg_in, ks.at[1], kr.at[1])
         r.encode_lent(["m", "e", "n", "f"])
+        r.Dp(3)
         r.encode_lent(["pm", "pe"])
         r.xrecv(2,"n")
         r.xrecv(3,"n")
@@ -806,8 +806,8 @@
         r.out_blocks(["f", "pm", "pe"])
         r.xrecv(0,"n")
         r.out_blocks(["pn"])
+        r.Df(1)
         r.Bp(1)
-        r.Df(1)
         r.Dp(0)
         r.xrecv(0,"f")
         r.out_blocks(["pf"])
@@ -817,10 +817,10 @@
         r.Dp(1)
         r.A(2)
         r.xrecv(1,"m")
+        r.query_blocks(["m", "e", "n", "f", "pm", "pe"])
         r.xrecv(1,"n")
-        r.query_blocks(["m", "e", "n", "f", "pm", "pe", "pn"])
         r.xrecv(1,"f")
-        r.query_blocks(["pf"])
+        r.query_blocks(["pn", "pf"])
         r.Be(2)
         r.C(2)
         r.A(3)
@@ -837,8 +837,8 @@
         r.xrecv(2,"m")
         r.xrecv(3,"m")
         r.encode(["pm", "pe"])
+        r.Dp(3)
         r.reduce_cores(["pm", "pe"])
-        r.Dp(3)
         r.xrecv(2,"n")
         r.xrecv(3,"n")
         r.xrecv(2,"f")
@@ -926,9 +926,9 @@
         r.query_blocks(["e", "pe", "m", "pm"])
         r.xrecv(1,"n")
         r.query_blocks(["n", "pn"])
+        r.C(2)
         r.xrecv(1,"f")
         r.query_blocks(["f", "pf"])
-        r.C(2)
         r.Cm(3)
         r.Bp(3)
         r.encode(["e", "pe", "m"])

time: 163 us -> 162 us (level)
  no operation moved by 1% of the time
where the time goes in v2:
time: 162 us; the launch traced here: 161 us
  Pallas kernels  161 us (99%)
    pallas_call x1, Pallas kernels, run_chain(): pl.pallas_call(functools.partial(chain_kernel, (q_rows, k_rows, depth //...  158 us

profile of v2, /device:TPU:0, one launch (start us, length us, event | category | flops | bytes accessed | tf_op | source)
XLA Modules:
  0.0 161.4 jit_solution(7704785238200219220)
XLA Ops:
  0.6 158.3 %shard_map.131 = (bf16[1,512,1024]{2,1,0:T(8,128)(2,1)}, bf16[768,512]{1,0:T(8,128)(2,1)}) custom-call(s32[2,2]{1,0:T(2,128)} %ql_hbm.1, s32[2,2]{1,0:T(2,128)} %ko_hbm.1, s32[2,2]{1,0:T(2,128)} %kl_hbm.1, s32[3,16]{1,0:T(4,128)} %bitcast.1, bf16[512,2048]{1,0:T(8,128)(2,1)} %top_hbm.1, bf16[1,512,1024]{2,1,0:T(8,128)(2,1)} %q_hbm.1, ...), custom_call_target="tpu_custom_call" | custom-call | tf_op jit(solution)/shard_map/pallas_call | solution.py:979
  158.9 2.3 %shard_map.132 = (bf16[1,512,1024]{2,1,0:T(8,128)(2,1)}, bf16[768,512]{1,0:T(8,128)(2,1)}) custom-call(bf16[1,512,1024]{2,1,0:T(8,128)(2,1)} %get-tuple-element.4.a_in, bf16[768,512]{1,0:T(8,128)(2,1)} %get-tuple-element.5.b_in), custom_call_target="tpu_custom_call" | custom-call | tf_op jit(solution)/shard_map/pallas_call | solution.py:1030

commit v3 on v2

--- a/solution.py
+++ b/solution.py
@@ -799,13 +799,11 @@
         r.Be(0)
         r.C(1)
         r.Be(1)
-        r.out_blocks(["m", "e", "n"])
         r.Bp(0)
         r.Df(0)
         r.xrecv(0,"m")
-        r.out_blocks(["f", "pm", "pe"])
         r.xrecv(0,"n")
-        r.out_blocks(["pn"])
+        r.out_blocks(["m", "e", "n", "f", "pm", "pe", "pn"])
         r.Df(1)
         r.Bp(1)
         r.Dp(0)
@@ -816,16 +814,17 @@
         r.attend()
         r.Dp(1)
         r.A(2)
+        r.query_blocks(["m", "e", "n"])
         r.xrecv(1,"m")
-        r.query_blocks(["m", "e", "n", "f", "pm", "pe"])
+        r.query_blocks(["f", "pm", "pe"])
         r.xrecv(1,"n")
         r.xrecv(1,"f")
         r.query_blocks(["pn", "pf"])
         r.Be(2)
         r.C(2)
         r.A(3)
+        r.section_blocks(["m", "e", "n", "f", "pm", "pe", "pn", "pf"])
         r.Df(2)
-        r.section_blocks(["m", "e", "n", "f", "pm", "pe", "pn", "pf"])
         r.Be(3)
         r.C(3)
         r.Bp(2)

time: 162 us -> 161 us (level)
  no operation moved by 1% of the time
where the time goes in v3:
time: 161 us
  Pallas kernels  160 us (99%)
    pallas_call x1, Pallas kernels, run_chain(): pl.pallas_call(functools.partial(chain_kernel, (q_rows, k_rows, depth //...  158 us

profile of v3, /device:TPU:0, one launch (start us, length us, event | category | flops | bytes accessed | tf_op | source)
XLA Modules:
  0.0 161.2 jit_solution(11496773953720957035)
XLA Ops:
  0.6 158.1 %shard_map.131 = (bf16[1,512,1024]{2,1,0:T(8,128)(2,1)}, bf16[768,512]{1,0:T(8,128)(2,1)}) custom-call(s32[2,2]{1,0:T(2,128)} %ql_hbm.1, s32[2,2]{1,0:T(2,128)} %ko_hbm.1, s32[2,2]{1,0:T(2,128)} %kl_hbm.1, s32[3,16]{1,0:T(4,128)} %bitcast.1, bf16[512,2048]{1,0:T(8,128)(2,1)} %top_hbm.1, bf16[1,512,1024]{2,1,0:T(8,128)(2,1)} %q_hbm.1, ...), custom_call_target="tpu_custom_call" | custom-call | tf_op jit(solution)/shard_map/pallas_call | solution.py:978
  158.7 2.3 %shard_map.132 = (bf16[1,512,1024]{2,1,0:T(8,128)(2,1)}, bf16[768,512]{1,0:T(8,128)(2,1)}) custom-call(bf16[1,512,1024]{2,1,0:T(8,128)(2,1)} %get-tuple-element.4.a_in, bf16[768,512]{1,0:T(8,128)(2,1)} %get-tuple-element.5.b_in), custom_call_target="tpu_custom_call" | custom-call | tf_op jit(solution)/shard_map/pallas_call | solution.py:1029
